TPU v7x, 32 devices: a whole 2x2x4 slice. The times are simulated.
32 devices in a mesh: groups: 2 (over x), ha: 16 (over z, y, core).
Axes of the slice: x: 2, y: 2, z: 4, core: 2. Of those that a mesh axis runs over, the one named last changes fastest.
Arguments:
- coarse: bfloat16 [64, 8, 16, 16], P(None, 'groups', 'ha'), parts along dimension 1, may hold values from -6 to 6
- skip: bfloat16 [32, 16, 32, 32], P(None, 'groups', 'ha'), parts along dimension 1, may hold values from -6 to 6
- up_weight: bfloat16 [2, 2, 2, 64, 64], replicated, may hold values from -0.75 to 0.75
- up_bias: float32 [64], replicated, may hold values from -3 to 3
- conv1_weight: bfloat16 [3, 3, 3, 32, 96], replicated, may hold values from -0.125 to 0.125
- conv1_bias: float32 [32], replicated, may hold values from -3 to 3
- conv2_weight: bfloat16 [3, 3, 3, 32, 32], replicated, may hold values from -0.21875 to 0.21875
- conv2_bias: float32 [32], replicated, may hold values from -3 to 3
Outputs:
- decoded: bfloat16 [32, 16, 32, 32], P(None, 'groups', 'ha'), parts along dimension 1
There are 2 independent parts, one for each index of `groups`. A program takes and returns all parts, laid end to end along the dimension named above; an argument that names none is the same for every part. Nothing has to cross between parts.
All inputs are finite; a program needn't handle non-finite values.
Results may differ from a plain program's by a relative error of at most 0.005.
Values may be sent and summed in bfloat16 or wider, within the bound.
A program may use at most 64 MiB of HBM per device.

v0:
```python
import jax
import jax.numpy as jnp
from jax import lax
from jax.sharding import PartitionSpec as P


def with_halo(array, sides, width):
    for axis, dim in sides:
        count, length = (lax.axis_size(axis), array.shape[dim])
        up = [(i, (i + 1) % count) for i in range(count - 1)]
        down = [(j, i) for i, j in up]
        last = lax.slice_in_dim(array, length - width, length, axis=dim)
        first = lax.slice_in_dim(array, 0, width, axis=dim)
        before = lax.ppermute(last, axis, up)
        after = lax.ppermute(first, axis, down)
        array = jnp.concatenate([before, array, after], axis=dim)
    return array


def upsample(inputs, weight, bias):
    values = jnp.einsum("abcoi,idpq->odapbqc", weight, inputs, preferred_element_type=jnp.float32)
    channels = weight.shape[3]
    values = values.reshape(channels, 2 * inputs.shape[1], 2 * inputs.shape[2], 2 * inputs.shape[3])
    return (values + bias[:, None, None, None]).astype(jnp.bfloat16)


def convolve(inputs, weight, bias):
    result = lax.conv_general_dilated(
        inputs[None],
        weight,
        (1, 1, 1),
        ((1, 1), (0, 0), (1, 1)),
        dimension_numbers=("NCDHW", "DHWOI", "NCDHW"),
        preferred_element_type=jnp.float32,
    )[0]
    return jnp.maximum(result + bias[:, None, None, None], 0.0).astype(jnp.bfloat16)


def inside_rows(height_rows, margin_rows):
    row_index = (
        lax.axis_index("ha") * height_rows
        - margin_rows
        + jnp.arange(height_rows + 2 * margin_rows, dtype=jnp.int32)
    )
    return (row_index >= 0) & (row_index < lax.axis_size("ha") * height_rows)


def body(coarse, skip, up_weight, up_bias, conv1_weight, conv1_bias, conv2_weight, conv2_bias):
    margin_rows = 2
    height_rows = skip.shape[2]
    local_fine = upsample(coarse, jnp.transpose(up_weight, (0, 2, 1, 3, 4)), up_bias)
    moved = lax.all_to_all(local_fine, "ha", split_axis=3, concat_axis=2, tiled=True)
    joined = jnp.concatenate([jnp.swapaxes(moved, 2, 3), skip], axis=0)
    padded = with_halo(joined, (("ha", 2),), margin_rows)
    widened = convolve(padded, conv1_weight, conv1_bias)
    inside = inside_rows(height_rows, 1)
    padded_hidden = jnp.where(inside[None, None, :, None], widened, jnp.zeros((), jnp.bfloat16))
    return convolve(padded_hidden, conv2_weight, conv2_bias)


def solution(mesh):
    return jax.shard_map(
        body,
        mesh=mesh,
        in_specs=(
            P(None, "groups", "ha", None),
            P(None, "groups", "ha", None),
            P(),
            P(),
            P(),
            P(),
            P(),
            P(),
        ),
        out_specs=P(None, "groups", "ha", None),
        check_vma=False,
    )
```

profile of v0, /device:TPU:8, one launch (start us, length us, event | category | flops | bytes accessed | tf_op | source)
XLA Modules:
  0.0 30.1 jit_solution(8856422117125722591)
XLA Ops:
  0.0 0.0 copy-start
  0.0 0.0 copy-start.2
  0.0 1.2 %convolution_bitcast_fusion = f32[64,4,2,1,2,16,2]{0,5,6,4,2,1,3:T(8,128)S(1)} fusion(bf16[64,4,1,16]{0,3,2,1:T(8,128)(2,1)} %param.8, bf16[2,2,2,64,64]{4,3,2,1,0:T(8,128)(2,1)} %param.10), kind=kOutput, calls=%fused_computation.6 | convolution fusion | flops 4194304 | bytes 204800 | tf_op jit(solution)/shard_map/abcoi,idpq->odapbqc/dot_general | solution.py:21
  1.2 0.1 copy.22
  1.4 0.0 copy-done.2
  1.4 0.0 copy-start.1
  1.4 0.1 copy.39
  1.5 0.8 %reshape.36 = bf16[16,2,1024]{2,1,0:T(2,128)(2,1)} reshape(bf16[32,8,2,64]{3,2,1,0:T(2,128)(2,1)S(1)} %bitcast.58) | data formatting | bytes 131072
  2.3 6.3 %all-to-all-start = ((bf16[16,2,1024]{2,1,0:T(2,128)(2,1)}), bf16[16,2,1024]{2,1,0:T(2,128)(2,1)S(1)}, u32[]{:S(2)}, u32[]{:S(2)}) async-start(bf16[16,2,1024]{2,1,0:T(2,128)(2,1)} %reshape.36), calls=%async_computation | async-start | bytes 131072 | tf_op jit(solution)/shard_map/all_to_all | solution.py:52
  8.6 0.0 copy-done.1
  8.6 0.2 copy.26
  8.8 4.9 %all-to-all-done = bf16[16,2,1024]{2,1,0:T(2,128)(2,1)S(1)} async-done(((bf16[16,2,1024]{2,1,0:T(2,128)(2,1)}), bf16[16,2,1024]{2,1,0:T(2,128)(2,1)S(1)}, u32[]{:S(2)}, u32[]{:S(2)}) %all-to-all-start) | async-done | bytes 65568 | tf_op jit(solution)/shard_map/all_to_all | solution.py:52
  13.7 0.1 reshape.37
  13.9 0.1 pad_maximum_fusion
  14.0 3.1 %collective-permute-start.1 = (bf16[96,8,2,32]{0,1,2,3:T(8,128)(2,1)S(1)}, bf16[96,8,2,32]{0,1,2,3:T(8,128)(2,1)S(1)}, u32[]{:S(2)}, u32[]{:S(2)}) collective-permute-start(bf16[96,8,2,32]{0,1,2,3:T(8,128)(2,1)S(1)} %pad_maximum_fusion), channel_id=1, source_target_pairs={{1,0},{2,1},{3,2},{4,3},{5,4},{6,5},{7,6},{8,7},{9,8},{10,9},{11,1... | collective-permute-start | bytes 294920 | tf_op jit(solution)/shard_map/ppermute | solution.py:15
  17.1 1.9 %collective-permute-start = (bf16[96,8,2,32]{0,1,2,3:T(8,128)(2,1)S(1)}, bf16[96,8,2,32]{0,1,2,3:T(8,128)(2,1)S(1)}, u32[]{:S(2)}, u32[]{:S(2)}) collective-permute-start(bf16[96,8,2,32]{0,1,2,3:T(8,128)(2,1)S(1)} %pad_maximum_fusion), channel_id=1, source_target_pairs={{0,1},{1,2},{2,3},{3,4},{4,5},{5,6},{6,7},{7,8},{8,9},{9,10},{10,1... | collective-permute-start | bytes 294920 | tf_op jit(solution)/shard_map/ppermute | solution.py:14
  19.0 0.6 %collective-permute-done.1 = bf16[96,8,2,32]{0,1,2,3:T(8,128)(2,1)S(1)} collective-permute-done((bf16[96,8,2,32]{0,1,2,3:T(8,128)(2,1)S(1)}, bf16[96,8,2,32]{0,1,2,3:T(8,128)(2,1)S(1)}, u32[]{:S(2)}, u32[]{:S(2)}) %collective-permute-start.1) | collective-permute-done | bytes 98336 | tf_op jit(solution)/shard_map/ppermute | solution.py:15
  19.6 4.7 %collective-permute-done = bf16[96,8,2,32]{0,1,2,3:T(8,128)(2,1)S(1)} collective-permute-done((bf16[96,8,2,32]{0,1,2,3:T(8,128)(2,1)S(1)}, bf16[96,8,2,32]{0,1,2,3:T(8,128)(2,1)S(1)}, u32[]{:S(2)}, u32[]{:S(2)}) %collective-permute-start) | collective-permute-done | bytes 98336 | tf_op jit(solution)/shard_map/ppermute | solution.py:14
  24.3 0.1 maximum_bitcast_fusion
  24.4 0.1 copy.33
  24.5 0.1 pad.clone
  24.6 0.0 copy-start.5
  24.6 0.0 copy-start.6
  24.6 0.1 copy.29
  24.7 0.1 slice.4
  24.7 0.0 copy-done
  24.8 0.5 %copy-done.5 = f32[32]{0:T(128)S(1)} copy-done((f32[32]{0:T(128)S(1)}, f32[32]{0:T(128)}, u32[]{:S(2)}) %copy-start.5) | copy-done | bytes 152
  25.2 0.0 copy-done.6
  25.3 0.0 copy-start.4
  25.3 2.4 %fusion.6 = bf16[8,4,1,8,5,32]{5,3,4,1,0,2:T(8,128)(2,1)S(1)} fusion(bf16[3,3,3,32,96]{4,3,2,1,0:T(8,128)(2,1)S(1)} %copy-done, bf16[96,8,6,1,7,2]{0,4,5,2,1,3:T(8,128)(2,1)S(1)} %slice.4, bf16[96,8,6,1,8,5]{0,4,5,2,1,3:T(8,128)(2,1)S(1)} %copy.29, f32[32]{0:T(128)S(1)} %copy-done.5, pred[4]{0:T(512)(128)(4,1)S(1)} %compare_and_fusion, ...), kind=kOutput, calls=%fused_computation.9 | convolution fusion | flops 196435968 | bytes 745644 | tf_op jit(solution)/shard_map/conv_general_dilated | solution.py:28
  27.8 0.0 copy-done.4
  27.8 0.8 %fusion.17 = f32[8,2,8,5,32]{4,2,3,1,0:T(8,128)S(1)} fusion(bf16[3,3,3,32,32]{4,3,2,1,0:T(8,128)(2,1)S(1)} %copy-done.4, bf16[8,4,1,7,1,32]{5,3,4,1,0,2:T(8,128)(2,1)S(1)} %get-tuple-element.6, bf16[8,4,1,7,1,32]{5,3,4,1,0,2:T(8,128)(2,1)S(1)} %get-tuple-element.5, bf16[8,4,1,8,5,32]{5,3,4,1,0,2:T(8,128)(2,1)S(1)} %fusion.6), kind=kOutput, calls=%fused_computation.21 | convolution fusion | flops 33013760 | bytes 247808 | tf_op jit(solution)/shard_map/conv_general_dilated | solution.py:28
  28.6 0.0 copy-start.3
  28.6 0.1 copy.30
  28.7 0.5 %copy-done.3 = f32[32]{0:T(128)S(1)} copy-done((f32[32]{0:T(128)S(1)}, f32[32]{0:T(128)}, u32[]{:S(2)}) %copy-start.3) | copy-done | bytes 152
  29.3 0.8 %copy.31 = bf16[32,8,2,32]{3,2,1,0:T(2,128)(2,1)} copy(bf16[32,8,2,32]{0,1,3,2:T(8,128)(2,1)S(1)} %fusion.29) | data formatting | bytes 65536 | tf_op jit(solution)/shard_map/convert_element_type | solution.py:36
  (6 shorter events, 0.1 us)
Async XLA Ops:
  0.0 24.7 %copy-start = (bf16[3,3,3,32,96]{4,3,2,1,0:T(8,128)(2,1)S(1)}, bf16[3,3,3,32,96]{4,3,2,1,0:T(8,128)(2,1)}, u32[]{:S(2)}) copy-start(bf16[3,3,3,32,96]{4,3,2,1,0:T(8,128)(2,1)} %param.12) | copy-start | bytes 497668
  0.0 1.4 %copy-start.2 = (f32[64]{0:T(128)S(1)}, f32[64]{0:T(128)}, u32[]{:S(2)}) copy-start(f32[64]{0:T(128)} %param.11) | copy-start | bytes 772
  1.4 7.2 %copy-start.1 = (bf16[32,8,2,32]{3,2,1,0:T(2,128)(2,1)S(1)}, bf16[32,8,2,32]{3,2,1,0:T(2,128)(2,1)}, u32[]{:S(2)}) copy-start(bf16[32,8,2,32]{3,2,1,0:T(2,128)(2,1)} %param.9) | copy-start | bytes 98308
  2.3 11.4 %all-to-all-start = ((bf16[16,2,1024]{2,1,0:T(2,128)(2,1)}), bf16[16,2,1024]{2,1,0:T(2,128)(2,1)S(1)}, u32[]{:S(2)}, u32[]{:S(2)}) async-start(bf16[16,2,1024]{2,1,0:T(2,128)(2,1)} %reshape.36), calls=%async_computation | async-start | bytes 131072 | tf_op jit(solution)/shard_map/all_to_all | solution.py:52
  14.0 5.6 %collective-permute-start.1 = (bf16[96,8,2,32]{0,1,2,3:T(8,128)(2,1)S(1)}, bf16[96,8,2,32]{0,1,2,3:T(8,128)(2,1)S(1)}, u32[]{:S(2)}, u32[]{:S(2)}) collective-permute-start(bf16[96,8,2,32]{0,1,2,3:T(8,128)(2,1)S(1)} %pad_maximum_fusion), channel_id=1, source_target_pairs={{1,0},{2,1},{3,2},{4,3},{5,4},{6,5},{7,6},{8,7},{9,8},{10,9},{11,1... | collective-permute-start | bytes 294920 | tf_op jit(solution)/shard_map/ppermute | solution.py:15
  17.1 7.2 %collective-permute-start = (bf16[96,8,2,32]{0,1,2,3:T(8,128)(2,1)S(1)}, bf16[96,8,2,32]{0,1,2,3:T(8,128)(2,1)S(1)}, u32[]{:S(2)}, u32[]{:S(2)}) collective-permute-start(bf16[96,8,2,32]{0,1,2,3:T(8,128)(2,1)S(1)} %pad_maximum_fusion), channel_id=1, source_target_pairs={{0,1},{1,2},{2,3},{3,4},{4,5},{5,6},{6,7},{7,8},{8,9},{9,10},{10,1... | collective-permute-start | bytes 294920 | tf_op jit(solution)/shard_map/ppermute | solution.py:14
  24.6 0.7 %copy-start.5 = (f32[32]{0:T(128)S(1)}, f32[32]{0:T(128)}, u32[]{:S(2)}) copy-start(f32[32]{0:T(128)} %param.13) | copy-start | bytes 388
  24.6 0.7 %copy-start.6 = (pred[8,5]{0,1:T(8,128)(4,1)S(1)}, pred[8,5]{0,1:T(8,128)(4,1)}, u32[]{:S(2)}) copy-start(pred[8,5]{0,1:T(8,128)(4,1)} %constant.27) | copy-start | bytes 124
  25.3 2.5 %copy-start.4 = (bf16[3,3,3,32,32]{4,3,2,1,0:T(8,128)(2,1)S(1)}, bf16[3,3,3,32,32]{4,3,2,1,0:T(8,128)(2,1)}, u32[]{:S(2)}) copy-start(bf16[3,3,3,32,32]{4,3,2,1,0:T(8,128)(2,1)} %param.14) | copy-start | bytes 165892
  28.6 0.7 %copy-start.3 = (f32[32]{0:T(128)S(1)}, f32[32]{0:T(128)}, u32[]{:S(2)}) copy-start(f32[32]{0:T(128)} %param.15) | copy-start | bytes 388
where the time goes:
time: 30.4 us; the launch traced here: 30.1 us
  starting transfers between devices  11.3 us (37%)
  waiting for transfers between devices  10.1 us (33%)
  matrix products  4.48 us (15%)
  local copies, waits for them, and re-layouts  3.7 us (12%)
    all_to_all x1, starting transfers between devices, body(): lax.all_to_all(local_fine, 'ha', split_axis=3, concat_axis=2, tiled=True)  6.3 us
    all_to_all x1, waiting for transfers between devices, body(): lax.all_to_all(local_fine, 'ha', split_axis=3, concat_axis=2, tiled=True)  4.9 us
    ppermute x1, waiting for transfers between devices, with_halo(): before = lax.ppermute(last, axis, up)  4.69 us
    conv_general_dilated x2, matrix products, convolve(): lax.conv_general_dilated(inputs[None], weight, (1, 1, 1), ((1, 1), (0, 0)...  3.26 us
    ppermute x1, starting transfers between devices, with_halo(): after = lax.ppermute(first, axis, down)  3.09 us
    unnamed x18, local copies, waits for them, and re-layouts  2.25 us
    ppermute x1, starting transfers between devices, with_halo(): before = lax.ppermute(last, axis, up)  1.92 us
    dot_general x1, matrix products, upsample(): jnp.einsum('abcoi,idpq->odapbqc', weight, inputs, preferred_element_type=...  1.22 us
  transfers between devices with their start and end apart: 3, of which 3 were waited for; matrix products, arithmetic and copies ran while one was open for 1% of the time, Pallas kernels for 0%

commit v1 on v0

--- a/solution.py
+++ b/solution.py
@@ -1,7 +1,15 @@
+import functools
+
 import jax
 import jax.numpy as jnp
 from jax import lax
+from jax.experimental import pallas as pl
+from jax.experimental.pallas import tpu as pltpu
 from jax.sharding import PartitionSpec as P
+
+VMEM_BUDGET = 40 * 1024 * 1024
+MARGIN = 2
+ROW_TILE = 16
 
 
 def with_halo(array, sides, width):
@@ -45,7 +53,7 @@
     return (row_index >= 0) & (row_index < lax.axis_size("ha") * height_rows)
 
 
-def body(coarse, skip, up_weight, up_bias, conv1_weight, conv1_bias, conv2_weight, conv2_bias):
+def large_body(coarse, skip, up_weight, up_bias, conv1_weight, conv1_bias, conv2_weight, conv2_bias):
     margin_rows = 2
     height_rows = skip.shape[2]
     local_fine = upsample(coarse, jnp.transpose(up_weight, (0, 2, 1, 3, 4)), up_bias)
@@ -58,6 +66,233 @@
     return convolve(padded_hidden, conv2_weight, conv2_bias)
 
 
+def iota(shape, dim):
+    return lax.broadcasted_iota(jnp.int32, shape, dim)
+
+
+def column(row):
+    size = row.shape[1]
+    same = iota((size, size), 0) == iota((size, size), 1)
+    return jnp.sum(jnp.where(same, row, 0.0), axis=1, keepdims=True)
+
+
+def one_hot(wanted, count):
+    return jnp.where(iota((wanted.shape[0], count), 1) == wanted, 1.0, 0.0).astype(jnp.bfloat16)
+
+
+def nt_dot(a, b):
+    return lax.dot_general(a, b, (((1,), (1,)), ((), ())), preferred_element_type=jnp.float32)
+
+
+def nn_dot(a, b):
+    return lax.dot_general(a, b, (((1,), (0,)), ((), ())), preferred_element_type=jnp.float32)
+
+
+def shifted_sum(weights, inputs_ref, rows_out, plane, fine_w, fine_d, outc):
+    parts = [[None] * 9 for _ in range(rows_out)]
+    for y in range(rows_out + 2):
+        taps = nn_dot(weights, inputs_ref[:, y * plane : (y + 1) * plane])
+        for q in range(3):
+            t = y - q
+            if 0 <= t < rows_out:
+                for p in range(3):
+                    for r in range(3):
+                        at = ((p * 3 + q) * 3 + r) * outc
+                        term = taps[at : at + outc]
+                        old = parts[t][p * 3 + r]
+                        parts[t][p * 3 + r] = term if old is None else old + term
+    lane = iota((1, plane), 1)
+    x, z = lax.rem(lane, fine_w), lax.div(lane, fine_w)
+    results = []
+    for t in range(rows_out):
+        planes = []
+        for p in range(3):
+            before, here, after = parts[t][3 * p : 3 * p + 3]
+            here = here + jnp.where(x > 0, pltpu.roll(before, 1, 1), 0.0)
+            here = here + jnp.where(x < fine_w - 1, pltpu.roll(after, plane - 1, 1), 0.0)
+            planes.append(here)
+        total = planes[1]
+        total = total + jnp.where(z > 0, pltpu.roll(planes[0], fine_w, 1), 0.0)
+        total = total + jnp.where(z < fine_d - 1, pltpu.roll(planes[2], plane - fine_w, 1), 0.0)
+        results.append(total)
+    return results
+
+
+def kernel(
+    n, depth, width, height, slab,
+    coarse_ref, skip_ref, upw_hbm, upb_ref, w1_hbm, b1_ref, w2_hbm, b2_ref,
+    out_ref,
+    outgoing, incoming, joined, hidden, upw_ref, w1_ref, w2_ref,
+    coarse_send, coarse_recv, skip_send, skip_recv, load_sem,
+):
+    me = lax.axis_index("ha")
+    cup = upw_ref.shape[1]
+    outc, skipc = out_ref.shape[0], skip_ref.shape[0]
+    near = height // n
+    own = 2 * near
+    local_w = width // n
+    fine_w, fine_d = 2 * width, 2 * depth
+    plane = fine_w * fine_d
+
+    barrier = pltpu.get_barrier_semaphore()
+    for k in range(1, n):
+        pl.semaphore_signal(
+            barrier, inc=1, device_id={"ha": lax.rem(me + k, n)}, device_id_type=pl.DeviceIdType.MESH
+        )
+    loads = [
+        pltpu.make_async_copy(src, dst, load_sem.at[i])
+        for i, (src, dst) in enumerate(((upw_hbm, upw_ref), (w1_hbm, w1_ref), (w2_hbm, w2_ref)))
+    ]
+    for load in loads:
+        load.start()
+    own_skip = pltpu.make_async_copy(
+        skip_ref, joined.at[pl.ds(cup, skipc), pl.ds(MARGIN * plane, own * plane)], load_sem.at[3]
+    )
+    own_skip.start()
+
+    at = iota((n * slab, 1), 0)
+    to, slot = lax.div(at, slab), lax.rem(at, slab)
+    row = to * near - 1 + lax.div(slot, depth * local_w)
+    wanted = (lax.rem(lax.div(slot, local_w), depth) * local_w + lax.rem(slot, local_w)) * height + row
+    real = (row >= 0) & (row < height) & (slot < (near + 2) * depth * local_w)
+    picked = nn_dot(one_hot(jnp.where(real, wanted, -1), depth * local_w * height), coarse_ref[...])
+    outgoing[...] = picked.astype(jnp.bfloat16).reshape(n, slab, cup)
+
+    pl.semaphore_wait(barrier, n - 1)
+
+    edge = MARGIN * plane
+    above = pltpu.make_async_remote_copy(
+        src_ref=skip_ref.at[:, pl.ds(0, edge)],
+        dst_ref=joined.at[pl.ds(cup, skipc), pl.ds((MARGIN + own) * plane, edge)],
+        send_sem=skip_send.at[0], recv_sem=skip_recv.at[0],
+        device_id={"ha": jnp.maximum(me - 1, 0)}, device_id_type=pl.DeviceIdType.MESH,
+    )
+    below = pltpu.make_async_remote_copy(
+        src_ref=skip_ref.at[:, pl.ds((own - MARGIN) * plane, edge)],
+        dst_ref=joined.at[pl.ds(cup, skipc), pl.ds(0, edge)],
+        send_sem=skip_send.at[1], recv_sem=skip_recv.at[1],
+        device_id={"ha": jnp.minimum(me + 1, n - 1)}, device_id_type=pl.DeviceIdType.MESH,
+    )
+    for k in range(1, n):
+        to = lax.rem(me + (n // 2 + k - 1) % (n - 1) + 1, n)
+        pltpu.make_async_remote_copy(
+            src_ref=outgoing.at[to], dst_ref=incoming.at[me],
+            send_sem=coarse_send, recv_sem=coarse_recv,
+            device_id={"ha": to}, device_id_type=pl.DeviceIdType.MESH,
+        ).start()
+    pl.when(me > 0)(above.start)
+    pl.when(me < n - 1)(below.start)
+    pltpu.make_async_copy(outgoing.at[me], incoming.at[me], coarse_recv).start()
+
+    at = iota(((near + 2) * plane, 1), 0)
+    h, z, w = lax.div(at, plane), lax.rem(lax.div(at, fine_w), fine_d), lax.div(lax.rem(at, fine_w), 2)
+    source = one_hot(
+        lax.div(w, local_w) * slab + (h * depth + lax.div(z, 2)) * local_w + lax.rem(w, local_w), n * slab
+    )
+    lane = iota((1, plane), 1)
+    odd_x = lax.rem(lane, 2) == 1
+    odd_z = lax.rem(lax.div(lane, fine_w), 2) == 1
+    up_bias, bias1, bias2 = column(upb_ref[...]), column(b1_ref[...]), column(b2_ref[...])
+
+    def inside(row):
+        return (me * own + row >= 0) & (me * own + row < n * own)
+
+    @pl.when(me == 0)
+    def _():
+        joined[cup:, : MARGIN * plane] = jnp.zeros((skipc, MARGIN * plane), jnp.bfloat16)
+
+    @pl.when(me == n - 1)
+    def _():
+        joined[cup:, (MARGIN + own) * plane :] = jnp.zeros((skipc, MARGIN * plane), jnp.bfloat16)
+
+    for load in loads:
+        load.wait()
+    pltpu.make_async_copy(incoming, incoming, coarse_recv).wait()
+
+    spread = nn_dot(source, incoming[...].reshape(n * slab, cup)).astype(jnp.bfloat16)
+    for h in range(near + 2):
+        taps = nt_dot(upw_ref[...], spread[h * plane : (h + 1) * plane])
+        for b in range(2):
+            def tap(a, c):
+                at = ((a * 2 + b) * 2 + c) * cup
+                return taps[at : at + cup]
+
+            even = jnp.where(odd_x, tap(0, 1), tap(0, 0))
+            odd = jnp.where(odd_x, tap(1, 1), tap(1, 0))
+            values = jnp.where(odd_z, odd, even) + up_bias
+            y = 2 * h + b
+            values = jnp.where(inside(y - MARGIN), values, 0.0)
+            joined[:cup, y * plane : (y + 1) * plane] = values.astype(jnp.bfloat16)
+
+    own_skip.wait()
+    pl.when(me < n - 1)(above.wait_recv)
+    pl.when(me > 0)(below.wait_recv)
+
+    for t, total in enumerate(shifted_sum(w1_ref[...], joined, own + 2, plane, fine_w, fine_d, outc)):
+        values = jnp.where(inside(t - 1), jnp.maximum(total + bias1, 0.0), 0.0)
+        hidden[:, t * plane : (t + 1) * plane] = values.astype(jnp.bfloat16)
+    for t, total in enumerate(shifted_sum(w2_ref[...], hidden, own, plane, fine_w, fine_d, outc)):
+        out_ref[:, t * plane : (t + 1) * plane] = jnp.maximum(total + bias2, 0.0).astype(jnp.bfloat16)
+
+    pl.when(me > 0)(above.wait_send)
+    pl.when(me < n - 1)(below.wait_send)
+    pltpu.make_async_copy(outgoing.at[pl.ds(0, n - 1)], incoming.at[pl.ds(0, n - 1)], coarse_send).wait()
+
+
+def body(coarse, skip, up_weight, up_bias, conv1_weight, conv1_bias, conv2_weight, conv2_bias):
+    n = lax.axis_size("ha")
+    cup, depth, local_w, height = coarse.shape
+    skipc, fine_d, own, fine_w = skip.shape
+    outc = conv1_weight.shape[3]
+    near = height // n
+    width = local_w * n
+    plane = fine_d * fine_w
+    slab = -(-((near + 2) * depth * local_w) // ROW_TILE) * ROW_TILE
+    taps = 27 * outc * plane * 4
+    need = (near + 2) * plane * (n * slab * 6 + 4 * 8 * cup) + (own + 4) * taps
+    if need > VMEM_BUDGET or plane % 128 or near < 1 or own < MARGIN:
+        return large_body(
+            coarse, skip, up_weight, up_bias, conv1_weight, conv1_bias, conv2_weight, conv2_bias
+        )
+    vmem, hbm = pl.BlockSpec(memory_space=pltpu.VMEM), pl.BlockSpec(memory_space=pl.ANY)
+    upw = up_weight.reshape(8 * cup, cup)
+    w1 = conv1_weight.reshape(27 * outc, cup + skipc)
+    w2 = conv2_weight.reshape(27 * outc, outc)
+    out = pl.pallas_call(
+        functools.partial(kernel, n, depth, width, height, slab),
+        out_shape=jax.ShapeDtypeStruct((outc, own * plane), jnp.bfloat16),
+        in_specs=[vmem, vmem, hbm, vmem, hbm, vmem, hbm, vmem],
+        out_specs=vmem,
+        scratch_shapes=[
+            pltpu.VMEM((n, slab, cup), jnp.bfloat16),
+            pltpu.VMEM((n, slab, cup), jnp.bfloat16),
+            pltpu.VMEM((cup + skipc, (own + 2 * MARGIN) * plane), jnp.bfloat16),
+            pltpu.VMEM((outc, (own + 2) * plane), jnp.bfloat16),
+            pltpu.VMEM(upw.shape, jnp.bfloat16),
+            pltpu.VMEM(w1.shape, jnp.bfloat16),
+            pltpu.VMEM(w2.shape, jnp.bfloat16),
+            pltpu.SemaphoreType.DMA,
+            pltpu.SemaphoreType.DMA,
+            pltpu.SemaphoreType.DMA((2,)),
+            pltpu.SemaphoreType.DMA((2,)),
+            pltpu.SemaphoreType.DMA((4,)),
+        ],
+        compiler_params=pltpu.CompilerParams(
+            collective_id=0, has_side_effects=True, vmem_limit_bytes=VMEM_BUDGET
+        ),
+    )(
+        jnp.transpose(coarse, (1, 2, 3, 0)).reshape(depth * local_w * height, cup),
+        jnp.swapaxes(skip, 1, 2).reshape(skipc, own * plane),
+        upw,
+        up_bias[None],
+        w1,
+        conv1_bias[None],
+        w2,
+        conv2_bias[None],
+    )
+    return jnp.swapaxes(out.reshape(outc, own, fine_d, fine_w), 1, 2)
+
+
 def solution(mesh):
     return jax.shard_map(
         body,

time: 30.4 us -> 15.6 us (0.51)
  the two profiles are of different devices: /device:TPU:8 before, /device:TPU:0 now
where the time goes in v1:
time: 15.6 us; the launch traced here: 15.4 us
  Pallas kernels  11.6 us (74%)
  local copies, waits for them, and re-layouts  3.66 us (23%)
    pallas_call x1, Pallas kernels, body(): pl.pallas_call(functools.partial(kernel, n, depth, width, height, slab),...  11.6 us
    unnamed x14, local copies, waits for them, and re-layouts  1.65 us
    transpose x1, local copies, waits for them, and re-layouts, body(): jnp.swapaxes(skip, 1, 2).reshape(skipc, own * plane)  0.96 us
    reshape x2, local copies, waits for them, and re-layouts, body(): return jnp.swapaxes(out.reshape(outc, own, fine_d, fine_w), 1, 2)  0.89 us

profile of v1, /device:TPU:0, one launch (start us, length us, event | category | flops | bytes accessed | tf_op | source)
XLA Modules:
  0.0 15.4 jit_solution(10072714099143919216)
XLA Ops:
  0.0 0.0 copy-start
  0.0 1.0 %copy.9 = bf16[32,2,8,32]{3,2,1,0:T(8,128)(2,1)S(1)} copy(bf16[32,2,8,32]{3,1,2,0:T(2,128)(2,1)} %bitcast.22) | data formatting | bytes 65536 | tf_op jit(solution)/shard_map/transpose | solution.py:285
  1.0 0.0 copy-start.2
  1.0 0.0 copy-start.3
  1.0 0.0 copy-start.4
  1.0 0.0 copy-start.5
  1.0 0.0 copy-start.6
  1.0 0.2 %reshape.19.skip_ref = bf16[32,512]{1,0:T(8,128)(2,1)S(1)} reshape(bf16[32,2,8,32]{3,2,1,0:T(8,128)(2,1)S(1)} %copy.9) | data formatting | bytes 65536 | tf_op jit(solution)/shard_map/reshape | solution.py:285
  1.2 0.0 copy-done
  1.2 0.7 %copy-done.2 = bf16[2,2,2,64,64]{4,3,2,1,0:T(8,128)(2,1)S(1)} copy-done((bf16[2,2,2,64,64]{4,3,2,1,0:T(8,128)(2,1)S(1)}, bf16[2,2,2,64,64]{4,3,2,1,0:T(8,128)(2,1)}, u32[]{:S(2)}) %copy-start.2) | copy-done | bytes 65560
  1.9 0.0 copy-done.3
  1.9 0.0 copy-done.4
  1.9 0.0 copy-done.5
  1.9 0.0 copy-done.6
  1.9 0.0 copy-start.1
  1.9 0.9 %copy-done.1 = bf16[3,3,3,32,32]{4,3,2,1,0:T(8,128)(2,1)S(1)} copy-done((bf16[3,3,3,32,32]{4,3,2,1,0:T(8,128)(2,1)S(1)}, bf16[3,3,3,32,32]{4,3,2,1,0:T(8,128)(2,1)}, u32[]{:S(2)}) %copy-start.1) | copy-done | bytes 55320
  2.8 11.6 %shard_map.82 = bf16[32,512]{1,0:T(8,128)(2,1)S(1)} custom-call(bf16[64,64]{1,0:T(8,128)(2,1)S(1)} %bitcast.18, bf16[32,512]{1,0:T(8,128)(2,1)S(1)} %reshape.19.skip_ref, bf16[512,64]{1,0:T(8,128)(2,1)S(1)} %bitcast.17, f32[1,64]{1,0:T(1,128)S(1)} %bitcast.19, bf16[864,96]{1,0:T(8,128)(2,1)S(1)} %bitcast.15, f32[1,32]{1,0:T(1,128)S(1)} %bitcast.20, ...), custom_call_target="tpu_custom_call" | custom-call | tf_op jit(solution)/shard_map/pallas_call | solution.py:261
  14.5 0.1 reshape.23
  14.6 0.8 %copy.12 = bf16[32,2,8,32]{3,1,2,0:T(2,128)(2,1)} copy(bf16[32,2,8,32]{3,2,1,0:T(8,128)(2,1)S(1)} %reshape.23) | data formatting | bytes 65536 | tf_op jit(solution)/shard_map/reshape | solution.py:293
Async XLA Ops:
  0.0 1.2 %copy-start = (bf16[3,3,3,32,96]{4,3,2,1,0:T(8,128)(2,1)S(1)}, bf16[3,3,3,32,96]{4,3,2,1,0:T(8,128)(2,1)}, u32[]{:S(2)}) copy-start(bf16[3,3,3,32,96]{4,3,2,1,0:T(8,128)(2,1)} %param.12) | copy-start | bytes 497668
  1.0 0.9 %copy-start.2 = (bf16[2,2,2,64,64]{4,3,2,1,0:T(8,128)(2,1)S(1)}, bf16[2,2,2,64,64]{4,3,2,1,0:T(8,128)(2,1)}, u32[]{:S(2)}) copy-start(bf16[2,2,2,64,64]{4,3,2,1,0:T(8,128)(2,1)} %param.10) | copy-start | bytes 196612
  1.0 0.9 %copy-start.3 = (bf16[64,4,1,16]{0,3,2,1:T(8,128)(2,1)S(1)}, bf16[64,4,1,16]{0,3,2,1:T(8,128)(2,1)}, u32[]{:S(2)}) copy-start(bf16[64,4,1,16]{0,3,2,1:T(8,128)(2,1)} %param.8) | copy-start | bytes 24580
  1.0 0.9 %copy-start.4 = (f32[64]{0:T(128)S(1)}, f32[64]{0:T(128)}, u32[]{:S(2)}) copy-start(f32[64]{0:T(128)} %param.11) | copy-start | bytes 772
  1.0 0.9 %copy-start.5 = (f32[32]{0:T(128)S(1)}, f32[32]{0:T(128)}, u32[]{:S(2)}) copy-start(f32[32]{0:T(128)} %param.13) | copy-start | bytes 388
  1.0 0.9 %copy-start.6 = (f32[32]{0:T(128)S(1)}, f32[32]{0:T(128)}, u32[]{:S(2)}) copy-start(f32[32]{0:T(128)} %param.15) | copy-start | bytes 388
  1.9 0.9 %copy-start.1 = (bf16[3,3,3,32,32]{4,3,2,1,0:T(8,128)(2,1)S(1)}, bf16[3,3,3,32,32]{4,3,2,1,0:T(8,128)(2,1)}, u32[]{:S(2)}) copy-start(bf16[3,3,3,32,32]{4,3,2,1,0:T(8,128)(2,1)} %param.14) | copy-start | bytes 165892

commit v2 on v0

--- a/solution.py
+++ b/solution.py
@@ -1,7 +1,16 @@
+import functools
+
 import jax
 import jax.numpy as jnp
 from jax import lax
+from jax.experimental import pallas as pl
+from jax.experimental.pallas import tpu as pltpu
 from jax.sharding import PartitionSpec as P
+
+VMEM_BUDGET = 40 * 1024 * 1024
+VMEM_LIMIT = 60 * 1024 * 1024
+MARGIN = 2
+ROW_TILE = 16
 
 
 def with_halo(array, sides, width):
@@ -45,7 +54,7 @@
     return (row_index >= 0) & (row_index < lax.axis_size("ha") * height_rows)
 
 
-def body(coarse, skip, up_weight, up_bias, conv1_weight, conv1_bias, conv2_weight, conv2_bias):
+def large_body(coarse, skip, up_weight, up_bias, conv1_weight, conv1_bias, conv2_weight, conv2_bias):
     margin_rows = 2
     height_rows = skip.shape[2]
     local_fine = upsample(coarse, jnp.transpose(up_weight, (0, 2, 1, 3, 4)), up_bias)
@@ -58,6 +67,275 @@
     return convolve(padded_hidden, conv2_weight, conv2_bias)
 
 
+def iota(shape, dim):
+    return lax.broadcasted_iota(jnp.int32, shape, dim)
+
+
+def column(row):
+    size = row.shape[1]
+    same = iota((size, size), 0) == iota((size, size), 1)
+    return jnp.sum(jnp.where(same, row, 0.0), axis=1, keepdims=True)
+
+
+def as_bits(mask):
+    return jnp.where(mask, 1.0, 0.0).astype(jnp.bfloat16)
+
+
+def one_hot(wanted, count):
+    return as_bits(iota((wanted.shape[0], count), 1) == wanted)
+
+
+def nt_dot(a, b):
+    return lax.dot_general(a, b, (((1,), (1,)), ((), ())), preferred_element_type=jnp.float32)
+
+
+def nn_dot(a, b):
+    return lax.dot_general(a, b, (((1,), (0,)), ((), ())), preferred_element_type=jnp.float32)
+
+
+def same_depth(channels, own, fine_d, fine_w):
+    row = iota((channels * fine_d * own, 1), 0)
+    lane = iota((1, fine_d * fine_w), 1)
+    return lax.rem(lax.div(row, own), fine_d) == lax.div(lane, fine_w)
+
+
+def width_tiles(fine_d, fine_w):
+    shape = (fine_w, fine_d * fine_w)
+    return as_bits(lax.rem(iota(shape, 1), fine_w) == iota(shape, 0))
+
+
+def planes_of(rows, channels, own, fine_d, fine_w):
+    wide = nn_dot(rows, width_tiles(fine_d, fine_w))
+    wide = jnp.where(same_depth(channels, own, fine_d, fine_w), wide, 0.0).astype(jnp.bfloat16)
+    at = iota((1, rows.shape[0]), 1)
+    goal = lax.rem(at, own) * channels + lax.div(at, own * fine_d)
+    return nn_dot(as_bits(iota((own * channels, 1), 0) == goal), wide).astype(jnp.bfloat16)
+
+
+def rows_of(planes, channels, own, fine_d, fine_w):
+    at = iota((channels * fine_d * own, 1), 0)
+    goal = lax.rem(at, own) * channels + lax.div(at, own * fine_d)
+    wide = nn_dot(one_hot(goal, own * channels), planes)
+    wide = jnp.where(same_depth(channels, own, fine_d, fine_w), wide, 0.0).astype(jnp.bfloat16)
+    return nt_dot(wide, width_tiles(fine_d, fine_w)).astype(jnp.bfloat16)
+
+
+def stack_height_taps(weights, outc):
+    block = 3 * outc
+    bands = []
+    for p in range(3):
+        taps = [weights[(p * 3 + q) * block : (p * 3 + q + 1) * block] for q in range(3)]
+        bands.append(jnp.concatenate(taps, axis=1))
+    return jnp.concatenate(bands, axis=0)
+
+
+def store_stacked(stacked_ref, values, y, rows_out, channels, first, plane):
+    for q in range(3):
+        t = y - q
+        if 0 <= t < rows_out:
+            at = q * channels + first
+            stacked_ref[at : at + values.shape[0], t * plane : (t + 1) * plane] = values
+
+
+def convolved_row(weights, inputs, fine_w, fine_d, outc):
+    plane = fine_w * fine_d
+    taps = nn_dot(weights, inputs)
+    lane = iota((1, plane), 1)
+    x, z = lax.rem(lane, fine_w), lax.div(lane, fine_w)
+    planes = []
+    for p in range(3):
+        before, here, after = (taps[(p * 3 + r) * outc : (p * 3 + r + 1) * outc] for r in range(3))
+        here = here + jnp.where(x > 0, pltpu.roll(before, 1, 1), 0.0)
+        here = here + jnp.where(x < fine_w - 1, pltpu.roll(after, plane - 1, 1), 0.0)
+        planes.append(here)
+    total = planes[1]
+    total = total + jnp.where(z > 0, pltpu.roll(planes[0], fine_w, 1), 0.0)
+    return total + jnp.where(z < fine_d - 1, pltpu.roll(planes[2], plane - fine_w, 1), 0.0)
+
+
+def kernel(
+    n, depth, width, height, slab,
+    coarse_hbm, skip_hbm, upw_hbm, upb_hbm, w1_hbm, b1_hbm, w2_hbm, b2_hbm,
+    out_ref,
+    coarse_ref, skip_ref, upw_ref, upb_ref, w1_ref, b1_ref, w2_ref, b2_ref,
+    outgoing, incoming, mine, theirs, joined, hidden,
+    coarse_send, coarse_recv, skip_send, skip_recv, load_sem,
+):
+    me = lax.axis_index("ha")
+    cup, outc = upw_ref.shape[1], w2_ref.shape[1]
+    skipc = w1_ref.shape[1] - cup
+    near = height // n
+    own = 2 * near
+    local_w = width // n
+    fine_w, fine_d = 2 * width, 2 * depth
+    plane = fine_w * fine_d
+    joint = cup + skipc
+
+    operands = (
+        (coarse_hbm, coarse_ref), (skip_hbm, skip_ref), (w1_hbm, w1_ref), (w2_hbm, w2_ref),
+        (upw_hbm, upw_ref), (upb_hbm, upb_ref), (b1_hbm, b1_ref), (b2_hbm, b2_ref),
+    )
+    loads = [pltpu.make_async_copy(src, dst, load_sem.at[i]) for i, (src, dst) in enumerate(operands)]
+    for load in loads[:2]:
+        load.start()
+    barrier = pltpu.get_barrier_semaphore()
+    for k in range(1, n):
+        pl.semaphore_signal(
+            barrier, inc=1, device_id={"ha": lax.rem(me + k, n)}, device_id_type=pl.DeviceIdType.MESH
+        )
+    for load in loads[2:]:
+        load.start()
+
+    at = iota((n * slab, 1), 0)
+    to, slot = lax.div(at, slab), lax.rem(at, slab)
+    row = to * near - 1 + lax.div(slot, depth * local_w)
+    wanted = (lax.rem(lax.div(slot, local_w), depth) * local_w + lax.rem(slot, local_w)) * height + row
+    real = (row >= 0) & (row < height) & (slot < (near + 2) * depth * local_w)
+    pick = one_hot(jnp.where(real, wanted, -1), depth * local_w * height)
+    loads[0].wait()
+    outgoing[...] = nn_dot(pick, coarse_ref[...]).astype(jnp.bfloat16).reshape(n, slab, cup)
+    loads[1].wait()
+    mine[...] = planes_of(skip_ref[...], skipc, own, fine_d, fine_w)
+
+    @pl.when(me == 0)
+    def _():
+        theirs[0] = jnp.zeros(theirs.shape[1:], theirs.dtype)
+
+    @pl.when(me == n - 1)
+    def _():
+        theirs[1] = jnp.zeros(theirs.shape[1:], theirs.dtype)
+
+    pl.semaphore_wait(barrier, n - 1)
+
+    edge = MARGIN * skipc
+    for k in range(1, n):
+        to = lax.rem(me + (n // 2 + k - 1) % (n - 1) + 1, n)
+        pltpu.make_async_remote_copy(
+            src_ref=outgoing.at[to], dst_ref=incoming.at[me],
+            send_sem=coarse_send, recv_sem=coarse_recv,
+            device_id={"ha": to}, device_id_type=pl.DeviceIdType.MESH,
+        ).start()
+    upward = pltpu.make_async_remote_copy(
+        src_ref=mine.at[pl.ds(0, edge)], dst_ref=theirs.at[1],
+        send_sem=skip_send.at[0], recv_sem=skip_recv.at[0],
+        device_id={"ha": jnp.maximum(me - 1, 0)}, device_id_type=pl.DeviceIdType.MESH,
+    )
+    downward = pltpu.make_async_remote_copy(
+        src_ref=mine.at[pl.ds((own - MARGIN) * skipc, edge)], dst_ref=theirs.at[0],
+        send_sem=skip_send.at[1], recv_sem=skip_recv.at[1],
+        device_id={"ha": jnp.minimum(me + 1, n - 1)}, device_id_type=pl.DeviceIdType.MESH,
+    )
+    pl.when(me > 0)(upward.start)
+    pl.when(me < n - 1)(downward.start)
+    pltpu.make_async_copy(outgoing.at[me], incoming.at[me], coarse_recv).start()
+
+    at = iota(((near + 2) * plane, 1), 0)
+    h, z, w = lax.div(at, plane), lax.rem(lax.div(at, fine_w), fine_d), lax.div(lax.rem(at, fine_w), 2)
+    source = one_hot(
+        lax.div(w, local_w) * slab + (h * depth + lax.div(z, 2)) * local_w + lax.rem(w, local_w), n * slab
+    )
+    lane = iota((1, plane), 1)
+    odd_x = lax.rem(lane, 2) == 1
+    odd_z = lax.rem(lax.div(lane, fine_w), 2) == 1
+    for load in loads[2:]:
+        load.wait()
+    weights1 = stack_height_taps(w1_ref[...], outc)
+    weights2 = stack_height_taps(w2_ref[...], outc)
+    up_bias, bias1, bias2 = column(upb_ref[...]), column(b1_ref[...]), column(b2_ref[...])
+
+    def inside(row):
+        return (me * own + row >= 0) & (me * own + row < n * own)
+
+    for y in range(own):
+        store_stacked(joined, mine[y * skipc : (y + 1) * skipc], y + MARGIN, own + 2, joint, cup, plane)
+    pl.when(me < n - 1)(upward.wait_recv)
+    pl.when(me > 0)(downward.wait_recv)
+    for y in range(MARGIN):
+        rows = slice(y * skipc, (y + 1) * skipc)
+        store_stacked(joined, theirs[0, rows], y, own + 2, joint, cup, plane)
+        store_stacked(joined, theirs[1, rows], y + MARGIN + own, own + 2, joint, cup, plane)
+    pltpu.make_async_copy(incoming, incoming, coarse_recv).wait()
+
+    spread = nn_dot(source, incoming[...].reshape(n * slab, cup)).astype(jnp.bfloat16)
+    for h in range(near + 2):
+        taps = nt_dot(upw_ref[...], spread[h * plane : (h + 1) * plane])
+        for b in range(2):
+            def tap(a, c):
+                at = ((a * 2 + b) * 2 + c) * cup
+                return taps[at : at + cup]
+
+            even = jnp.where(odd_x, tap(0, 1), tap(0, 0))
+            odd = jnp.where(odd_x, tap(1, 1), tap(1, 0))
+            values = jnp.where(odd_z, odd, even) + up_bias
+            y = 2 * h + b
+            values = jnp.where(inside(y - MARGIN), values, 0.0).astype(jnp.bfloat16)
+            store_stacked(joined, values, y, own + 2, joint, 0, plane)
+
+    for t in range(own + 2):
+        total = convolved_row(weights1, joined[:, t * plane : (t + 1) * plane], fine_w, fine_d, outc)
+        values = jnp.where(inside(t - 1), jnp.maximum(total + bias1, 0.0), 0.0).astype(jnp.bfloat16)
+        store_stacked(hidden, values, t, own, outc, 0, plane)
+    outs = []
+    for t in range(own):
+        total = convolved_row(weights2, hidden[:, t * plane : (t + 1) * plane], fine_w, fine_d, outc)
+        outs.append(jnp.maximum(total + bias2, 0.0).astype(jnp.bfloat16))
+    out_ref[...] = rows_of(jnp.concatenate(outs, axis=0), outc, own, fine_d, fine_w)
+
+    pl.when(me > 0)(upward.wait_send)
+    pl.when(me < n - 1)(downward.wait_send)
+    pltpu.make_async_copy(outgoing.at[pl.ds(0, n - 1)], incoming.at[pl.ds(0, n - 1)], coarse_send).wait()
+
+
+def body(coarse, skip, up_weight, up_bias, conv1_weight, conv1_bias, conv2_weight, conv2_bias):
+    n = lax.axis_size("ha")
+    cup, depth, local_w, height = coarse.shape
+    skipc, fine_d, own, fine_w = skip.shape
+    outc = conv1_weight.shape[3]
+    near = height // n
+    width = local_w * n
+    plane = fine_d * fine_w
+    slab = -(-((near + 2) * depth * local_w) // ROW_TILE) * ROW_TILE
+    need = (near + 2) * plane * (n * slab * 6 + 4 * 8 * cup) + (own + 4) * 27 * outc * plane * 4
+    if need > VMEM_BUDGET or plane % 128 or near < 1 or own < MARGIN:
+        return large_body(
+            coarse, skip, up_weight, up_bias, conv1_weight, conv1_bias, conv2_weight, conv2_bias
+        )
+    operands = (
+        jnp.transpose(coarse, (1, 2, 3, 0)).reshape(depth * local_w * height, cup),
+        skip.reshape(skipc * fine_d * own, fine_w),
+        up_weight.reshape(8 * cup, cup),
+        up_bias[None],
+        conv1_weight.reshape(27 * outc, cup + skipc),
+        conv1_bias[None],
+        conv2_weight.reshape(27 * outc, outc),
+        conv2_bias[None],
+    )
+    out = pl.pallas_call(
+        functools.partial(kernel, n, depth, width, height, slab),
+        out_shape=jax.ShapeDtypeStruct((outc * fine_d * own, fine_w), jnp.bfloat16),
+        in_specs=[pl.BlockSpec(memory_space=pltpu.HBM)] * len(operands),
+        out_specs=pl.BlockSpec(memory_space=pltpu.VMEM),
+        scratch_shapes=[pltpu.VMEM(operand.shape, operand.dtype) for operand in operands]
+        + [
+            pltpu.VMEM((n, slab, cup), jnp.bfloat16),
+            pltpu.VMEM((n, slab, cup), jnp.bfloat16),
+            pltpu.VMEM((own * skipc, plane), jnp.bfloat16),
+            pltpu.VMEM((2, MARGIN * skipc, plane), jnp.bfloat16),
+            pltpu.VMEM((3 * (cup + skipc), (own + 2) * plane), jnp.bfloat16),
+            pltpu.VMEM((3 * outc, own * plane), jnp.bfloat16),
+            pltpu.SemaphoreType.DMA,
+            pltpu.SemaphoreType.DMA,
+            pltpu.SemaphoreType.DMA((2,)),
+            pltpu.SemaphoreType.DMA((2,)),
+            pltpu.SemaphoreType.DMA((len(operands),)),
+        ],
+        compiler_params=pltpu.CompilerParams(
+            collective_id=0, has_side_effects=True, vmem_limit_bytes=VMEM_LIMIT
+        ),
+    )(*operands)
+    return out.reshape(outc, fine_d, own, fine_w)
+
+
 def solution(mesh):
     return jax.shard_map(
         body,

time: 30.4 us -> 13.7 us (0.45)
  the two profiles are of different devices: /device:TPU:8 before, /device:TPU:0 now
where the time goes in v2:
time: 13.7 us; the launch traced here: 13.5 us
  Pallas kernels  11.8 us (86%)
  local copies, waits for them, and re-layouts  1.65 us (12%)
    pallas_call x1, Pallas kernels, body(): pl.pallas_call(functools.partial(kernel, n, depth, width, height, slab),...  11.8 us
    unnamed x1, local copies, waits for them, and re-layouts  1.65 us

profile of v2, /device:TPU:0, one launch (start us, length us, event | category | flops | bytes accessed | tf_op | source)
XLA Modules:
  0.0 13.5 jit_solution(15145618504018326491)
XLA Ops:
  0.0 11.8 %shard_map.82 = bf16[512,32]{1,0:T(8,128)(2,1)} custom-call(bf16[64,64]{1,0:T(8,128)(2,1)} %bitcast.16, bf16[512,32]{1,0:T(8,128)(2,1)} %bitcast.14, bf16[512,64]{1,0:T(8,128)(2,1)} %bitcast.15, f32[1,64]{1,0:T(1,128)} %bitcast.17, bf16[864,96]{1,0:T(8,128)(2,1)} %bitcast.12, f32[1,32]{1,0:T(1,128)} %bitcast.18, bf16[864,32]{1,0:T(8,128)(2,1)} %bitcast.13, ...), custom_call_target="tpu_custom_call" | custom-call | tf_op jit(solution)/shard_map/pallas_call | solution.py:313
  11.8 1.7 %copy.10 = bf16[32,8,2,32]{3,2,1,0:T(2,128)(2,1)} copy(bf16[32,8,2,32]{3,2,1,0:T(2,128)(2,1)} %bitcast.11) | data formatting | bytes 65536

commit v3 on v2

--- a/solution.py
+++ b/solution.py
@@ -8,9 +8,10 @@
 from jax.sharding import PartitionSpec as P
 
 VMEM_BUDGET = 40 * 1024 * 1024
-VMEM_LIMIT = 60 * 1024 * 1024
+VMEM_LIMIT = 48 * 1024 * 1024
 MARGIN = 2
 ROW_TILE = 16
+UNROLL = 1
 
 
 def with_halo(array, sides, width):
@@ -112,34 +113,12 @@
     return nn_dot(as_bits(iota((own * channels, 1), 0) == goal), wide).astype(jnp.bfloat16)
 
 
-def rows_of(planes, channels, own, fine_d, fine_w):
-    at = iota((channels * fine_d * own, 1), 0)
-    goal = lax.rem(at, own) * channels + lax.div(at, own * fine_d)
-    wide = nn_dot(one_hot(goal, own * channels), planes)
-    wide = jnp.where(same_depth(channels, own, fine_d, fine_w), wide, 0.0).astype(jnp.bfloat16)
-    return nt_dot(wide, width_tiles(fine_d, fine_w)).astype(jnp.bfloat16)
-
-
-def stack_height_taps(weights, outc):
-    block = 3 * outc
-    bands = []
-    for p in range(3):
-        taps = [weights[(p * 3 + q) * block : (p * 3 + q + 1) * block] for q in range(3)]
-        bands.append(jnp.concatenate(taps, axis=1))
-    return jnp.concatenate(bands, axis=0)
-
-
-def store_stacked(stacked_ref, values, y, rows_out, channels, first, plane):
-    for q in range(3):
-        t = y - q
-        if 0 <= t < rows_out:
-            at = q * channels + first
-            stacked_ref[at : at + values.shape[0], t * plane : (t + 1) * plane] = values
-
-
-def convolved_row(weights, inputs, fine_w, fine_d, outc):
+def stack_taps(weights, pieces, lanes):
+    return jnp.concatenate([weights[at : at + size, lanes] for at, size in pieces], axis=1)
+
+
+def moved_sum(taps, fine_w, fine_d, outc):
     plane = fine_w * fine_d
-    taps = nn_dot(weights, inputs)
     lane = iota((1, plane), 1)
     x, z = lax.rem(lane, fine_w), lax.div(lane, fine_w)
     planes = []
@@ -153,12 +132,16 @@
     return total + jnp.where(z < fine_d - 1, pltpu.roll(planes[2], plane - fine_w, 1), 0.0)
 
 
+def rows_at(ref, index, size, count=None):
+    return ref.at[pl.ds(pl.multiple_of(index * size, size), size if count is None else count)]
+
+
 def kernel(
     n, depth, width, height, slab,
     coarse_hbm, skip_hbm, upw_hbm, upb_hbm, w1_hbm, b1_hbm, w2_hbm, b2_hbm,
     out_ref,
     coarse_ref, skip_ref, upw_ref, upb_ref, w1_ref, b1_ref, w2_ref, b2_ref,
-    outgoing, incoming, mine, theirs, joined, hidden,
+    outgoing, incoming, up_planes, skip_planes, hidden, outs, source, order, up_stack, up1, skip1, stack2, partial,
     coarse_send, coarse_recv, skip_send, skip_recv, load_sem,
 ):
     me = lax.axis_index("ha")
@@ -169,7 +152,7 @@
     local_w = width // n
     fine_w, fine_d = 2 * width, 2 * depth
     plane = fine_w * fine_d
-    joint = cup + skipc
+    reach = own + 2 * MARGIN
 
     operands = (
         (coarse_hbm, coarse_ref), (skip_hbm, skip_ref), (w1_hbm, w1_ref), (w2_hbm, w2_ref),
@@ -194,20 +177,8 @@
     pick = one_hot(jnp.where(real, wanted, -1), depth * local_w * height)
     loads[0].wait()
     outgoing[...] = nn_dot(pick, coarse_ref[...]).astype(jnp.bfloat16).reshape(n, slab, cup)
-    loads[1].wait()
-    mine[...] = planes_of(skip_ref[...], skipc, own, fine_d, fine_w)
-
-    @pl.when(me == 0)
-    def _():
-        theirs[0] = jnp.zeros(theirs.shape[1:], theirs.dtype)
-
-    @pl.when(me == n - 1)
-    def _():
-        theirs[1] = jnp.zeros(theirs.shape[1:], theirs.dtype)
-
     pl.semaphore_wait(barrier, n - 1)
 
-    edge = MARGIN * skipc
     for k in range(1, n):
         to = lax.rem(me + (n // 2 + k - 1) % (n - 1) + 1, n)
         pltpu.make_async_remote_copy(
@@ -215,71 +186,106 @@
             send_sem=coarse_send, recv_sem=coarse_recv,
             device_id={"ha": to}, device_id_type=pl.DeviceIdType.MESH,
         ).start()
+    pltpu.make_async_copy(outgoing.at[me], incoming.at[me], coarse_recv).start()
+
+    edge = MARGIN * skipc
+    loads[1].wait()
+    skip_planes[edge : edge + own * skipc] = planes_of(skip_ref[...], skipc, own, fine_d, fine_w)
     upward = pltpu.make_async_remote_copy(
-        src_ref=mine.at[pl.ds(0, edge)], dst_ref=theirs.at[1],
+        src_ref=skip_planes.at[pl.ds(edge, edge)], dst_ref=skip_planes.at[pl.ds((MARGIN + own) * skipc, edge)],
         send_sem=skip_send.at[0], recv_sem=skip_recv.at[0],
         device_id={"ha": jnp.maximum(me - 1, 0)}, device_id_type=pl.DeviceIdType.MESH,
     )
     downward = pltpu.make_async_remote_copy(
-        src_ref=mine.at[pl.ds((own - MARGIN) * skipc, edge)], dst_ref=theirs.at[0],
+        src_ref=skip_planes.at[pl.ds(own * skipc, edge)], dst_ref=skip_planes.at[pl.ds(0, edge)],
         send_sem=skip_send.at[1], recv_sem=skip_recv.at[1],
         device_id={"ha": jnp.minimum(me + 1, n - 1)}, device_id_type=pl.DeviceIdType.MESH,
     )
     pl.when(me > 0)(upward.start)
     pl.when(me < n - 1)(downward.start)
-    pltpu.make_async_copy(outgoing.at[me], incoming.at[me], coarse_recv).start()
-
-    at = iota(((near + 2) * plane, 1), 0)
-    h, z, w = lax.div(at, plane), lax.rem(lax.div(at, fine_w), fine_d), lax.div(lax.rem(at, fine_w), 2)
-    source = one_hot(
-        lax.div(w, local_w) * slab + (h * depth + lax.div(z, 2)) * local_w + lax.rem(w, local_w), n * slab
-    )
-    lane = iota((1, plane), 1)
-    odd_x = lax.rem(lane, 2) == 1
-    odd_z = lax.rem(lax.div(lane, fine_w), 2) == 1
+
+    @pl.when(me == 0)
+    def _():
+        skip_planes[:edge] = jnp.zeros((edge, plane), skip_planes.dtype)
+
+    @pl.when(me == n - 1)
+    def _():
+        skip_planes[(MARGIN + own) * skipc :] = jnp.zeros((edge, plane), skip_planes.dtype)
+
+    at = iota((plane, 1), 0)
+    z, x = lax.div(at, fine_w), lax.rem(at, fine_w)
+    w = lax.div(x, 2)
+    taken = lax.div(w, local_w) * slab + lax.div(z, 2) * local_w + lax.rem(w, local_w)
+    parity = lax.rem(z, 2) * 2 + lax.rem(x, 2)
+
+    def fill_source(h, _):
+        rows_at(source, h, plane)[...] = one_hot(taken + h * (depth * local_w), n * slab)
+
+    lax.fori_loop(0, near + 2, fill_source, None)
+
+    chunk = fine_d * own
+
+    def fill_order(o, _):
+        rows_at(order, o, chunk)[...] = one_hot(iota((chunk, 1), 0) * outc + o, chunk * outc)
+
+    lax.fori_loop(0, outc, fill_order, None)
+
     for load in loads[2:]:
         load.wait()
-    weights1 = stack_height_taps(w1_ref[...], outc)
-    weights2 = stack_height_taps(w2_ref[...], outc)
+    for b in range(2):
+        pieces = [(((a * 2 + b) * 2 + c) * cup, cup) for a in range(2) for c in range(2)]
+        up_stack[b * cup : (b + 1) * cup] = stack_taps(upw_ref, pieces, slice(None))
+    block = 3 * outc
+    for p in range(3):
+        pieces = [((p * 3 + q) * block, block) for q in range(3)]
+        rows = slice(p * block, (p + 1) * block)
+        up1[rows] = stack_taps(w1_ref, pieces, slice(0, cup))
+        skip1[rows] = stack_taps(w1_ref, pieces, slice(cup, cup + skipc))
+        stack2[rows] = stack_taps(w2_ref, pieces, slice(None))
     up_bias, bias1, bias2 = column(upb_ref[...]), column(b1_ref[...]), column(b2_ref[...])
+    up_bias = jnp.concatenate([up_bias, up_bias], axis=0)
 
     def inside(row):
         return (me * own + row >= 0) & (me * own + row < n * own)
 
-    for y in range(own):
-        store_stacked(joined, mine[y * skipc : (y + 1) * skipc], y + MARGIN, own + 2, joint, cup, plane)
     pl.when(me < n - 1)(upward.wait_recv)
     pl.when(me > 0)(downward.wait_recv)
-    for y in range(MARGIN):
-        rows = slice(y * skipc, (y + 1) * skipc)
-        store_stacked(joined, theirs[0, rows], y, own + 2, joint, cup, plane)
-        store_stacked(joined, theirs[1, rows], y + MARGIN + own, own + 2, joint, cup, plane)
+
+    def convolve_skip(t, _):
+        rows_at(partial, t, 9 * outc)[...] = nn_dot(skip1[...], rows_at(skip_planes, t, skipc, 3 * skipc)[...])
+
+    lax.fori_loop(0, own + 2, convolve_skip, None)
     pltpu.make_async_copy(incoming, incoming, coarse_recv).wait()
 
-    spread = nn_dot(source, incoming[...].reshape(n * slab, cup)).astype(jnp.bfloat16)
-    for h in range(near + 2):
-        taps = nt_dot(upw_ref[...], spread[h * plane : (h + 1) * plane])
-        for b in range(2):
-            def tap(a, c):
-                at = ((a * 2 + b) * 2 + c) * cup
-                return taps[at : at + cup]
-
-            even = jnp.where(odd_x, tap(0, 1), tap(0, 0))
-            odd = jnp.where(odd_x, tap(1, 1), tap(1, 0))
-            values = jnp.where(odd_z, odd, even) + up_bias
-            y = 2 * h + b
-            values = jnp.where(inside(y - MARGIN), values, 0.0).astype(jnp.bfloat16)
-            store_stacked(joined, values, y, own + 2, joint, 0, plane)
-
-    for t in range(own + 2):
-        total = convolved_row(weights1, joined[:, t * plane : (t + 1) * plane], fine_w, fine_d, outc)
-        values = jnp.where(inside(t - 1), jnp.maximum(total + bias1, 0.0), 0.0).astype(jnp.bfloat16)
-        store_stacked(hidden, values, t, own, outc, 0, plane)
-    outs = []
-    for t in range(own):
-        total = convolved_row(weights2, hidden[:, t * plane : (t + 1) * plane], fine_w, fine_d, outc)
-        outs.append(jnp.maximum(total + bias2, 0.0).astype(jnp.bfloat16))
-    out_ref[...] = rows_of(jnp.concatenate(outs, axis=0), outc, own, fine_d, fine_w)
+    received = incoming[...].reshape(n * slab, cup)
+    received = jnp.concatenate([received] * 4, axis=1)
+    mine = parity == lax.div(iota((1, 4 * cup), 1), cup)
+
+    def upsample_row(h, _):
+        spread = nn_dot(rows_at(source, h, plane)[...], received)
+        spread = jnp.where(mine, spread, 0.0).astype(jnp.bfloat16)
+        values = nt_dot(up_stack[...], spread) + up_bias
+        values = jnp.where(inside(2 * h - MARGIN), values, 0.0)
+        rows_at(up_planes, h, 2 * cup)[...] = values.astype(jnp.bfloat16)
+
+    lax.fori_loop(0, near + 2, upsample_row, None, unroll=UNROLL)
+
+    def convolve_joined(t, _):
+        taps = nn_dot(up1[...], rows_at(up_planes, t, cup, 3 * cup)[...]) + rows_at(partial, t, 9 * outc)[...]
+        values = jnp.maximum(moved_sum(taps, fine_w, fine_d, outc) + bias1, 0.0)
+        values = jnp.where(inside(t - 1), values, 0.0)
+        rows_at(hidden, t, outc)[...] = values.astype(jnp.bfloat16)
+
+    lax.fori_loop(0, own + 2, convolve_joined, None, unroll=UNROLL)
+
+    def convolve_hidden(t, _):
+        taps = nn_dot(stack2[...], rows_at(hidden, t, outc, 3 * outc)[...])
+        values = jnp.maximum(moved_sum(taps, fine_w, fine_d, outc) + bias2, 0.0)
+        rows_at(outs, t, outc)[...] = values.astype(jnp.bfloat16)
+
+    lax.fori_loop(0, own, convolve_hidden, None, unroll=UNROLL)
+    slices = [outs[:, z * fine_w : (z + 1) * fine_w] for z in range(fine_d)]
+    out_ref[...] = nn_dot(order[...], jnp.concatenate(slices, axis=0)).astype(jnp.bfloat16)
 
     pl.when(me > 0)(upward.wait_send)
     pl.when(me < n - 1)(downward.wait_send)
@@ -300,6 +306,7 @@
         return large_body(
             coarse, skip, up_weight, up_bias, conv1_weight, conv1_bias, conv2_weight, conv2_bias
         )
+    reach = own + 2 * MARGIN
     operands = (
         jnp.transpose(coarse, (1, 2, 3, 0)).reshape(depth * local_w * height, cup),
         skip.reshape(skipc * fine_d * own, fine_w),
@@ -312,17 +319,24 @@
     )
     out = pl.pallas_call(
         functools.partial(kernel, n, depth, width, height, slab),
-        out_shape=jax.ShapeDtypeStruct((outc * fine_d * own, fine_w), jnp.bfloat16),
+        out_shape=pltpu.VMEM((outc * fine_d * own, fine_w), jnp.bfloat16),
         in_specs=[pl.BlockSpec(memory_space=pltpu.HBM)] * len(operands),
         out_specs=pl.BlockSpec(memory_space=pltpu.VMEM),
         scratch_shapes=[pltpu.VMEM(operand.shape, operand.dtype) for operand in operands]
         + [
             pltpu.VMEM((n, slab, cup), jnp.bfloat16),
             pltpu.VMEM((n, slab, cup), jnp.bfloat16),
-            pltpu.VMEM((own * skipc, plane), jnp.bfloat16),
-            pltpu.VMEM((2, MARGIN * skipc, plane), jnp.bfloat16),
-            pltpu.VMEM((3 * (cup + skipc), (own + 2) * plane), jnp.bfloat16),
-            pltpu.VMEM((3 * outc, own * plane), jnp.bfloat16),
+            pltpu.VMEM((reach * cup, plane), jnp.bfloat16),
+            pltpu.VMEM((reach * skipc, plane), jnp.bfloat16),
+            pltpu.VMEM(((own + 2) * outc, plane), jnp.bfloat16),
+            pltpu.VMEM((own * outc, plane), jnp.bfloat16),
+            pltpu.VMEM(((near + 2) * plane, n * slab), jnp.bfloat16),
+            pltpu.VMEM((outc * fine_d * own, outc * fine_d * own), jnp.bfloat16),
+            pltpu.VMEM((2 * cup, 4 * cup), jnp.bfloat16),
+            pltpu.VMEM((9 * outc, 3 * cup), jnp.bfloat16),
+            pltpu.VMEM((9 * outc, 3 * skipc), jnp.bfloat16),
+            pltpu.VMEM((9 * outc, 3 * outc), jnp.bfloat16),
+            pltpu.VMEM(((own + 2) * 9 * outc, plane), jnp.float32),
             pltpu.SemaphoreType.DMA,
             pltpu.SemaphoreType.DMA,
             pltpu.SemaphoreType.DMA((2,)),
@@ -332,7 +346,7 @@
         compiler_params=pltpu.CompilerParams(
             collective_id=0, has_side_effects=True, vmem_limit_bytes=VMEM_LIMIT
         ),
-    )(*operands)
+    )(*(pltpu.with_memory_space_constraint(operand, pltpu.HBM) for operand in operands))
     return out.reshape(outc, fine_d, own, fine_w)
 
 

time: 13.7 us -> 13.9 us (1.015)
  the two profiles are of different devices: /device:TPU:0 before, /device:TPU:1 now
where the time goes in v3:
time: 13.9 us; the launch traced here: 13.7 us
  Pallas kernels  13 us (94%)
  local copies, waits for them, and re-layouts  0.66 us (5%)
    pallas_call x1, Pallas kernels, body(): pl.pallas_call(functools.partial(kernel, n, depth, width, height, slab),...  13 us
    unnamed x1, local copies, waits for them, and re-layouts  0.66 us

profile of v3, /device:TPU:1, one launch (start us, length us, event | category | flops | bytes accessed | tf_op | source)
XLA Modules:
  0.0 13.7 jit_solution(2455491177754312469)
XLA Ops:
  0.0 13.0 %shard_map.82 = bf16[512,32]{1,0:T(8,128)(2,1)S(1)} custom-call(bf16[64,64]{1,0:T(8,128)(2,1)} %bitcast.16, bf16[512,32]{1,0:T(8,128)(2,1)} %bitcast.14, bf16[512,64]{1,0:T(8,128)(2,1)} %bitcast.15, f32[1,64]{1,0:T(1,128)} %bitcast.17, bf16[864,96]{1,0:T(8,128)(2,1)} %bitcast.12, f32[1,32]{1,0:T(1,128)} %bitcast.18, bf16[864,32]{1,0:T(8,128)(2,1)} %bitcast.13, ...), custom_call_target="tpu_custom_call" | custom-call | tf_op jit(solution)/shard_map/pallas_call | solution.py:320
  13.0 0.7 %copy.10 = bf16[32,8,2,32]{3,2,1,0:T(2,128)(2,1)} copy(bf16[32,8,2,32]{3,2,1,0:T(2,128)(2,1)S(1)} %bitcast.11) | data formatting | bytes 65536

commit v4 on v3

--- a/solution.py
+++ b/solution.py
@@ -11,7 +11,6 @@
 VMEM_LIMIT = 48 * 1024 * 1024
 MARGIN = 2
 ROW_TILE = 16
-UNROLL = 1
 
 
 def with_halo(array, sides, width):
@@ -133,7 +132,8 @@
 
 
 def rows_at(ref, index, size, count=None):
-    return ref.at[pl.ds(pl.multiple_of(index * size, size), size if count is None else count)]
+    first = index * size if isinstance(index, int) else pl.multiple_of(index * size, size)
+    return ref.at[pl.ds(first, size if count is None else count)]
 
 
 def kernel(
@@ -221,7 +221,8 @@
     def fill_source(h, _):
         rows_at(source, h, plane)[...] = one_hot(taken + h * (depth * local_w), n * slab)
 
-    lax.fori_loop(0, near + 2, fill_source, None)
+    for i in range(near + 2):
+        fill_source(i, None)
 
     chunk = fine_d * own
 
@@ -254,7 +255,8 @@
     def convolve_skip(t, _):
         rows_at(partial, t, 9 * outc)[...] = nn_dot(skip1[...], rows_at(skip_planes, t, skipc, 3 * skipc)[...])
 
-    lax.fori_loop(0, own + 2, convolve_skip, None)
+    for i in range(own + 2):
+        convolve_skip(i, None)
     pltpu.make_async_copy(incoming, incoming, coarse_recv).wait()
 
     received = incoming[...].reshape(n * slab, cup)
@@ -268,7 +270,8 @@
         values = jnp.where(inside(2 * h - MARGIN), values, 0.0)
         rows_at(up_planes, h, 2 * cup)[...] = values.astype(jnp.bfloat16)
 
-    lax.fori_loop(0, near + 2, upsample_row, None, unroll=UNROLL)
+    for i in range(near + 2):
+        upsample_row(i, None)
 
     def convolve_joined(t, _):
         taps = nn_dot(up1[...], rows_at(up_planes, t, cup, 3 * cup)[...]) + rows_at(partial, t, 9 * outc)[...]
@@ -276,14 +279,16 @@
         values = jnp.where(inside(t - 1), values, 0.0)
         rows_at(hidden, t, outc)[...] = values.astype(jnp.bfloat16)
 
-    lax.fori_loop(0, own + 2, convolve_joined, None, unroll=UNROLL)
+    for i in range(own + 2):
+        convolve_joined(i, None)
 
     def convolve_hidden(t, _):
         taps = nn_dot(stack2[...], rows_at(hidden, t, outc, 3 * outc)[...])
         values = jnp.maximum(moved_sum(taps, fine_w, fine_d, outc) + bias2, 0.0)
         rows_at(outs, t, outc)[...] = values.astype(jnp.bfloat16)
 
-    lax.fori_loop(0, own, convolve_hidden, None, unroll=UNROLL)
+    for i in range(own):
+        convolve_hidden(i, None)
     slices = [outs[:, z * fine_w : (z + 1) * fine_w] for z in range(fine_d)]
     out_ref[...] = nn_dot(order[...], jnp.concatenate(slices, axis=0)).astype(jnp.bfloat16)
 

time: 13.9 us -> 11.7 us (0.84)
  the two profiles are of different devices: /device:TPU:1 before, /device:TPU:0 now
where the time goes in v4:
time: 11.7 us; the launch traced here: 11.5 us
  Pallas kernels  10.8 us (92%)
  local copies, waits for them, and re-layouts  0.66 us (6%)
    pallas_call x1, Pallas kernels, body(): pl.pallas_call(functools.partial(kernel, n, depth, width, height, slab),...  10.8 us
    unnamed x1, local copies, waits for them, and re-layouts  0.66 us

profile of v4, /device:TPU:0, one launch (start us, length us, event | category | flops | bytes accessed | tf_op | source)
XLA Modules:
  0.0 11.5 jit_solution(16289777182666280805)
XLA Ops:
  0.0 10.8 %shard_map.82 = bf16[512,32]{1,0:T(8,128)(2,1)S(1)} custom-call(bf16[64,64]{1,0:T(8,128)(2,1)} %bitcast.16, bf16[512,32]{1,0:T(8,128)(2,1)} %bitcast.14, bf16[512,64]{1,0:T(8,128)(2,1)} %bitcast.15, f32[1,64]{1,0:T(1,128)} %bitcast.17, bf16[864,96]{1,0:T(8,128)(2,1)} %bitcast.12, f32[1,32]{1,0:T(1,128)} %bitcast.18, bf16[864,32]{1,0:T(8,128)(2,1)} %bitcast.13, ...), custom_call_target="tpu_custom_call" | custom-call | tf_op jit(solution)/shard_map/pallas_call | solution.py:325
  10.9 0.7 %copy.10 = bf16[32,8,2,32]{3,2,1,0:T(2,128)(2,1)} copy(bf16[32,8,2,32]{3,2,1,0:T(2,128)(2,1)S(1)} %bitcast.11) | data formatting | bytes 65536

commit v5 on v4

--- a/solution.py
+++ b/solution.py
@@ -176,7 +176,8 @@
     real = (row >= 0) & (row < height) & (slot < (near + 2) * depth * local_w)
     pick = one_hot(jnp.where(real, wanted, -1), depth * local_w * height)
     loads[0].wait()
-    outgoing[...] = nn_dot(pick, coarse_ref[...]).astype(jnp.bfloat16).reshape(n, slab, cup)
+    twice = jnp.concatenate([coarse_ref[...]] * 2, axis=1)
+    outgoing[...] = nn_dot(pick, twice).astype(jnp.bfloat16).reshape(n, slab, 2 * cup)
     pl.semaphore_wait(barrier, n - 1)
 
     for k in range(1, n):
@@ -259,8 +260,8 @@
         convolve_skip(i, None)
     pltpu.make_async_copy(incoming, incoming, coarse_recv).wait()
 
-    received = incoming[...].reshape(n * slab, cup)
-    received = jnp.concatenate([received] * 4, axis=1)
+    received = incoming[...].reshape(n * slab, 2 * cup)
+    received = jnp.concatenate([received] * 2, axis=1)
     mine = parity == lax.div(iota((1, 4 * cup), 1), cup)
 
     def upsample_row(h, _):
@@ -329,8 +330,8 @@
         out_specs=pl.BlockSpec(memory_space=pltpu.VMEM),
         scratch_shapes=[pltpu.VMEM(operand.shape, operand.dtype) for operand in operands]
         + [
-            pltpu.VMEM((n, slab, cup), jnp.bfloat16),
-            pltpu.VMEM((n, slab, cup), jnp.bfloat16),
+            pltpu.VMEM((n, slab, 2 * cup), jnp.bfloat16),
+            pltpu.VMEM((n, slab, 2 * cup), jnp.bfloat16),
             pltpu.VMEM((reach * cup, plane), jnp.bfloat16),
             pltpu.VMEM((reach * skipc, plane), jnp.bfloat16),
             pltpu.VMEM(((own + 2) * outc, plane), jnp.bfloat16),

time: 11.7 us -> 11.7 us (level)
  no operation moved by 1% of the time
where the time goes in v5:
time: 11.7 us; the launch traced here: 11.4 us
  Pallas kernels  10.8 us (92%)
  local copies, waits for them, and re-layouts  0.66 us (6%)
    pallas_call x1, Pallas kernels, body(): pl.pallas_call(functools.partial(kernel, n, depth, width, height, slab),...  10.8 us
    unnamed x1, local copies, waits for them, and re-layouts  0.66 us

profile of v5, /device:TPU:0, one launch (start us, length us, event | category | flops | bytes accessed | tf_op | source)
XLA Modules:
  0.0 11.4 jit_solution(11443246844925269068)
XLA Ops:
  0.0 10.8 %shard_map.82 = bf16[512,32]{1,0:T(8,128)(2,1)S(1)} custom-call(bf16[64,64]{1,0:T(8,128)(2,1)} %bitcast.16, bf16[512,32]{1,0:T(8,128)(2,1)} %bitcast.14, bf16[512,64]{1,0:T(8,128)(2,1)} %bitcast.15, f32[1,64]{1,0:T(1,128)} %bitcast.17, bf16[864,96]{1,0:T(8,128)(2,1)} %bitcast.12, f32[1,32]{1,0:T(1,128)} %bitcast.18, bf16[864,32]{1,0:T(8,128)(2,1)} %bitcast.13, ...), custom_call_target="tpu_custom_call" | custom-call | tf_op jit(solution)/shard_map/pallas_call | solution.py:326
  10.8 0.7 %copy.10 = bf16[32,8,2,32]{3,2,1,0:T(2,128)(2,1)} copy(bf16[32,8,2,32]{3,2,1,0:T(2,128)(2,1)S(1)} %bitcast.11) | data formatting | bytes 65536

commit v6 on v5

--- a/solution.py
+++ b/solution.py
@@ -141,7 +141,7 @@
     coarse_hbm, skip_hbm, upw_hbm, upb_hbm, w1_hbm, b1_hbm, w2_hbm, b2_hbm,
     out_ref,
     coarse_ref, skip_ref, upw_ref, upb_ref, w1_ref, b1_ref, w2_ref, b2_ref,
-    outgoing, incoming, up_planes, skip_planes, hidden, outs, source, order, up_stack, up1, skip1, stack2, partial,
+    outgoing, incoming, up_planes, skip_planes, hidden, source, up_stack, up1, skip1, stack2, partial,
     coarse_send, coarse_recv, skip_send, skip_recv, load_sem,
 ):
     me = lax.axis_index("ha")
@@ -224,13 +224,6 @@
 
     for i in range(near + 2):
         fill_source(i, None)
-
-    chunk = fine_d * own
-
-    def fill_order(o, _):
-        rows_at(order, o, chunk)[...] = one_hot(iota((chunk, 1), 0) * outc + o, chunk * outc)
-
-    lax.fori_loop(0, outc, fill_order, None)
 
     for load in loads[2:]:
         load.wait()
@@ -286,12 +279,10 @@
     def convolve_hidden(t, _):
         taps = nn_dot(stack2[...], rows_at(hidden, t, outc, 3 * outc)[...])
         values = jnp.maximum(moved_sum(taps, fine_w, fine_d, outc) + bias2, 0.0)
-        rows_at(outs, t, outc)[...] = values.astype(jnp.bfloat16)
+        out_ref[:, t * plane : (t + 1) * plane] = values.astype(jnp.bfloat16)
 
     for i in range(own):
         convolve_hidden(i, None)
-    slices = [outs[:, z * fine_w : (z + 1) * fine_w] for z in range(fine_d)]
-    out_ref[...] = nn_dot(order[...], jnp.concatenate(slices, axis=0)).astype(jnp.bfloat16)
 
     pl.when(me > 0)(upward.wait_send)
     pl.when(me < n - 1)(downward.wait_send)
@@ -325,7 +316,7 @@
     )
     out = pl.pallas_call(
         functools.partial(kernel, n, depth, width, height, slab),
-        out_shape=pltpu.VMEM((outc * fine_d * own, fine_w), jnp.bfloat16),
+        out_shape=pltpu.VMEM((outc, own * plane), jnp.bfloat16),
         in_specs=[pl.BlockSpec(memory_space=pltpu.HBM)] * len(operands),
         out_specs=pl.BlockSpec(memory_space=pltpu.VMEM),
         scratch_shapes=[pltpu.VMEM(operand.shape, operand.dtype) for operand in operands]
@@ -335,9 +326,7 @@
             pltpu.VMEM((reach * cup, plane), jnp.bfloat16),
             pltpu.VMEM((reach * skipc, plane), jnp.bfloat16),
             pltpu.VMEM(((own + 2) * outc, plane), jnp.bfloat16),
-            pltpu.VMEM((own * outc, plane), jnp.bfloat16),
             pltpu.VMEM(((near + 2) * plane, n * slab), jnp.bfloat16),
-            pltpu.VMEM((outc * fine_d * own, outc * fine_d * own), jnp.bfloat16),
             pltpu.VMEM((2 * cup, 4 * cup), jnp.bfloat16),
             pltpu.VMEM((9 * outc, 3 * cup), jnp.bfloat16),
             pltpu.VMEM((9 * outc, 3 * skipc), jnp.bfloat16),
@@ -353,7 +342,7 @@
             collective_id=0, has_side_effects=True, vmem_limit_bytes=VMEM_LIMIT
         ),
     )(*(pltpu.with_memory_space_constraint(operand, pltpu.HBM) for operand in operands))
-    return out.reshape(outc, fine_d, own, fine_w)
+    return jnp.swapaxes(out.reshape(outc, own, fine_d, fine_w), 1, 2)
 
 
 def solution(mesh):

time: 11.7 us -> 11.5 us (0.983)
  Pallas kernels: 10.8 us -> 10.4 us
  local copies, waits for them, and re-layouts: 0.66 us -> 0.89 us
    reshape x0 -> x2, local copies, waits for them, and re-layouts: none -> 0.89 us  [body(): return jnp.swapaxes(out.reshape(outc, own, fine_d, fine_w), 1, 2)]
    unnamed x1 -> x0, local copies, waits for them, and re-layouts: 0.66 us -> none
    pallas_call x1, Pallas kernels: 10.8 us -> 10.4 us  [body(): pl.pallas_call(functools.partial(kernel, n, depth, width, height, slab),...]
where the time goes in v6:
time: 11.5 us; the launch traced here: 11.3 us
  Pallas kernels  10.4 us (90%)
  local copies, waits for them, and re-layouts  0.89 us (8%)
    pallas_call x1, Pallas kernels, body(): pl.pallas_call(functools.partial(kernel, n, depth, width, height, slab),...  10.4 us
    reshape x2, local copies, waits for them, and re-layouts, body(): return jnp.swapaxes(out.reshape(outc, own, fine_d, fine_w), 1, 2)  0.89 us

profile of v6, /device:TPU:0, one launch (start us, length us, event | category | flops | bytes accessed | tf_op | source)
XLA Modules:
  0.0 11.3 jit_solution(15681580405120259382)
XLA Ops:
  0.0 10.4 %shard_map.82 = bf16[32,512]{1,0:T(8,128)(2,1)S(1)} custom-call(bf16[64,64]{1,0:T(8,128)(2,1)} %bitcast.17, bf16[512,32]{1,0:T(8,128)(2,1)} %bitcast.15, bf16[512,64]{1,0:T(8,128)(2,1)} %bitcast.16, f32[1,64]{1,0:T(1,128)} %bitcast.18, bf16[864,96]{1,0:T(8,128)(2,1)} %bitcast.13, f32[1,32]{1,0:T(1,128)} %bitcast.19, bf16[864,32]{1,0:T(8,128)(2,1)} %bitcast.14, ...), custom_call_target="tpu_custom_call" | custom-call | tf_op jit(solution)/shard_map/pallas_call | solution.py:317
  10.4 0.1 %reshape.23 = bf16[32,2,8,32]{3,2,1,0:T(8,128)(2,1)S(1)} reshape(bf16[32,512]{1,0:T(8,128)(2,1)S(1)} %shard_map.82) | data formatting | bytes 65536 | tf_op jit(solution)/shard_map/reshape | solution.py:345
  10.6 0.8 %copy.11 = bf16[32,2,8,32]{3,1,2,0:T(2,128)(2,1)} copy(bf16[32,2,8,32]{3,2,1,0:T(8,128)(2,1)S(1)} %reshape.23) | data formatting | bytes 65536 | tf_op jit(solution)/shard_map/reshape | solution.py:345
